TPU v7x, 512 devices: a whole 4x4x16 slice. The times are simulated.
512 devices in a mesh: orb: 64 (over z_hi, x, y), dom: 8 (over z_lo, core).
Axes of the slice: x: 4, y: 4, z: 16 (z_hi: 4, z_lo: 4; z = z_hi * 4 + z_lo), core: 2. Of those that a mesh axis runs over, the one named last changes fastest.
Arguments:
- orbitals: float32 [64, 2, 96, 128, 128], P('orb', None, 'dom'), may hold values from -7 to 7, as said below
- occupations: float32 [64], P('orb'), may hold values from 0.5 to 2
- potential: float32 [96, 128, 128], P('dom'), may hold values from -4 to 4
Outputs:
- new_orbitals: float32 [64, 2, 96, 128, 128], P('orb', None, 'dom')
- hartree: float32 [96, 128, 128], P('dom', 'orb')
Inputs may be any that keep to these rules, and one draw needn't show every extreme that they name: `orbitals`: real and imaginary parts of order one.
All inputs are finite; a program needn't handle non-finite values.
Results may differ from a plain program's by a relative error of at most 0.0018.
Values sent between devices are 32-bit elements; how exact they have to be, the bound alone decides.
A program may use at most 64 MiB of HBM per device.

v0:
```python
import math

import jax
import jax.numpy as jnp
from jax import lax
from jax.sharding import PartitionSpec as P

NY = 128
NZ = 128
TERMS = 4


SPACING = 0.4
TIME_STEP = 0.03
STENCIL = (-205.0 / 72.0, 8.0 / 5.0, -1.0 / 5.0, 8.0 / 315.0, -1.0 / 560.0)
HIGHEST = lax.Precision.HIGHEST


def with_halo(cells, sides, width):
    for axis, dim in sides:
        count = lax.axis_size(axis)
        ends = count - 1
        head = lax.slice_in_dim(cells, 0, width, axis=dim)
        tail = lax.slice_in_dim(cells, cells.shape[dim] - width, cells.shape[dim], axis=dim)
        cells = jnp.concatenate(
            [
                lax.ppermute(tail, axis, [(i, (i + 1) % count) for i in range(ends)]),
                cells,
                lax.ppermute(head, axis, [((i + 1) % count, i) for i in range(ends)]),
            ],
            axis=dim,
        )
    return cells


def laplacian_rows(padded):
    rows = padded.shape[2] - 8
    across = padded.shape[3]
    along = padded.shape[4]
    full = jnp.pad(padded, ((0, 0), (0, 0), (0, 0), (4, 4), (4, 4)))
    total = 3.0 * STENCIL[0] * full[:, :, 4 : 4 + rows, 4 : 4 + across, 4 : 4 + along]
    for reach in range(1, 5):
        pairs = (
            full[:, :, 4 + reach : 4 + reach + rows, 4 : 4 + across, 4 : 4 + along]
            + full[:, :, 4 - reach : 4 - reach + rows, 4 : 4 + across, 4 : 4 + along]
        )
        pairs = (
            pairs
            + full[:, :, 4 : 4 + rows, 4 + reach : 4 + reach + across, 4 : 4 + along]
            + full[:, :, 4 : 4 + rows, 4 - reach : 4 - reach + across, 4 : 4 + along]
        )
        pairs = (
            pairs
            + full[:, :, 4 : 4 + rows, 4 : 4 + across, 4 + reach : 4 + reach + along]
            + full[:, :, 4 : 4 + rows, 4 : 4 + across, 4 - reach : 4 - reach + along]
        )
        total = total + STENCIL[reach] * pairs
    return total / (SPACING * SPACING)


def next_term(padded, potential_rows, order):
    rows = padded.shape[2] - 8
    center = padded[:, :, 4 : 4 + rows]
    applied = -0.5 * laplacian_rows(padded) + potential_rows * center
    return TIME_STEP / order * jnp.stack([applied[:, 1], -applied[:, 0]], axis=1)


def wave_squares(index, length):
    signed = jnp.minimum(index, length - index).astype(jnp.float32)
    scaled = signed * (2.0 * math.pi / (length * SPACING))
    return scaled * scaled


def dft_tables(length):
    index = jnp.arange(length, dtype=jnp.int32)
    phase = index[:, None] * index[None, :] % length
    angle = phase.astype(jnp.float32) * (2.0 * math.pi / length)
    return (jnp.cos(angle), jnp.sin(angle))


def third_section(real_y, imag_y, cos_z, sin_z):
    real_part = jnp.einsum("kxz,zw->kxw", real_y, cos_z, precision=HIGHEST) + jnp.einsum(
        "kxz,zw->kxw", imag_y, sin_z, precision=HIGHEST
    )
    imag_part = jnp.einsum("kxz,zw->kxw", imag_y, cos_z, precision=HIGHEST) - jnp.einsum(
        "kxz,zw->kxw", real_y, sin_z, precision=HIGHEST
    )
    return jnp.stack([real_part, imag_part], axis=1)


def body(orbitals, occupations, potential):
    groups = lax.axis_size("orb")
    potential_full = potential[None, None]
    term = orbitals
    result = orbitals
    for order in range(1, TERMS):
        padded = with_halo(term, (("dom", 2),), 4)
        term = next_term(padded, potential_full, order)
        result = result + term
    squares_local = result[:, 0] * result[:, 0] + result[:, 1] * result[:, 1]
    density_part = jnp.sum(occupations[:, None, None, None] * squares_local, axis=0) / math.sqrt(
        orbitals.shape[0] * groups
    )
    cos_y, sin_y = dft_tables(NY)
    cos_z, sin_z = dft_tables(NZ)
    lines = NY // groups
    own_start = lax.axis_index("orb") * lines
    rows_cos = cos_y
    rows_sin = sin_y
    real_y = jnp.einsum("ky,xyz->kxz", rows_cos, density_part, precision=HIGHEST)
    imag_y = -jnp.einsum("ky,xyz->kxz", rows_sin, density_part, precision=HIGHEST)
    modes = lax.psum_scatter(
        third_section(real_y, imag_y, cos_z, sin_z), "orb", scatter_dimension=0, tiled=True
    )
    pencils = lax.all_to_all(modes, "dom", split_axis=3, concat_axis=2, tiled=True)
    full_x = pencils.shape[2]
    slab_z = pencils.shape[3]
    cos_x, sin_x = dft_tables(full_x)
    real_in = pencils[:, 0]
    imag_in = pencils[:, 1]
    fwd_real = jnp.einsum("kx,yxz->ykz", cos_x, real_in, precision=HIGHEST) + jnp.einsum(
        "kx,yxz->ykz", sin_x, imag_in, precision=HIGHEST
    )
    fwd_imag = jnp.einsum("kx,yxz->ykz", cos_x, imag_in, precision=HIGHEST) - jnp.einsum(
        "kx,yxz->ykz", sin_x, real_in, precision=HIGHEST
    )
    wave_y = wave_squares(own_start + jnp.arange(lines, dtype=jnp.int32), NY)
    wave_x = wave_squares(jnp.arange(full_x, dtype=jnp.int32), full_x)
    wave_z = wave_squares(lax.axis_index("dom") * slab_z + jnp.arange(slab_z, dtype=jnp.int32), NZ)
    squares = wave_y[:, None, None] + wave_x[None, :, None] + wave_z[None, None, :]
    kernel = jnp.where(squares > 0.0, 4.0 * math.pi / jnp.where(squares > 0.0, squares, 1.0), 0.0)
    solved_real = kernel * fwd_real
    solved_imag = kernel * fwd_imag
    back_real = jnp.einsum("kx,ykz->yxz", cos_x, solved_real, precision=HIGHEST) - jnp.einsum(
        "kx,ykz->yxz", sin_x, solved_imag, precision=HIGHEST
    )
    back_imag = jnp.einsum("kx,ykz->yxz", sin_x, solved_real, precision=HIGHEST) + jnp.einsum(
        "kx,ykz->yxz", cos_x, solved_imag, precision=HIGHEST
    )
    returned = lax.all_to_all(
        jnp.stack([back_real, back_imag], axis=1), "dom", split_axis=2, concat_axis=3, tiled=True
    )
    scale = 1.0 / (full_x * NY * NZ)
    count = returned.shape[0]
    real_part = returned[:, 0]
    imag_part = returned[:, 1]
    z_real = jnp.einsum("yxk,kz->yxz", real_part, cos_z, precision=HIGHEST) - jnp.einsum(
        "yxk,kz->yxz", imag_part, sin_z, precision=HIGHEST
    )
    z_imag = jnp.einsum("yxk,kz->yxz", real_part, sin_z, precision=HIGHEST) + jnp.einsum(
        "yxk,kz->yxz", imag_part, cos_z, precision=HIGHEST
    )
    rows_cos = lax.dynamic_slice_in_dim(cos_y, own_start, count, 0)
    rows_sin = lax.dynamic_slice_in_dim(sin_y, own_start, count, 0)
    field = jnp.einsum("kw,kxz->xwz", rows_cos, z_real, precision=HIGHEST) - jnp.einsum(
        "kw,kxz->xwz", rows_sin, z_imag, precision=HIGHEST
    )
    share = field * scale
    hartree = lax.psum_scatter(share, "orb", scatter_dimension=1, tiled=True)
    return (result, hartree)


def solution(mesh):
    return jax.shard_map(
        body,
        mesh=mesh,
        in_specs=(P("orb", None, "dom", None, None), P("orb"), P("dom", None, None)),
        out_specs=(P("orb", None, "dom", None, None), P("dom", "orb", None)),
        check_vma=False,
    )
```

profile of v0, /device:TPU:6, one launch (start us, length us, event | category | flops | bytes accessed | tf_op | source)
XLA Modules:
  0.0 1462.0 jit_solution(2403588148311827656)
XLA Ops:
  7.2 1.4 fusion.275
  8.6 1.8 collective-permute-start.1
  10.4 1.3 collective-permute-start
  12.3 1.3 copy-done.1
  13.6 2.2 collective-permute-done
  15.9 2.3 select_maximum_fusion.4
  18.2 8.3 fusion.70
  26.9 1.4 collective-permute-start.2
  28.3 9.8 collective-permute-start.3
  38.1 1.4 broadcast_multiply_fusion
  39.6 3.9 select_maximum_fusion.2
  43.4 26.9 %fusion.43 = f32[1,2,12,128,128]{4,3,2,1,0:T(8,128)} fusion(f32[1,2,12,128,128]{4,3,2,1,0:T(8,128)S(1)} %fusion.83, f32[1,2,4,128,128]{4,3,2,1,0:T(8,128)} %copy-done.10, f32[1,2,4,128,128]{4,3,2,1,0:T(8,128)} %copy-done.8, f32[1,2,20,136,136]{4,3,2,1,0:T(8,128)} %select_maximum_fusion.2, f32[1,1,12,128,128]{4,3,2,1,0:T(8,128)S(1)} %get-tuple-element.21, ...), kind=kLoop, calls=%fused_computation.77 | loop fusion | flops 16121856 | bytes 31719424 | tf_op jit(solution)/shard_map/add | solution.py:64
  70.4 1.5 fusion.272
  72.1 0.7 copy-done.2
  73.1 1.3 collective-permute-start.4
  74.4 9.1 collective-permute-start.5
  84.2 0.6 collective-permute-done.5
  84.8 3.9 select_maximum_fusion
  88.7 27.3 %fusion.13 = f32[1,2,12,128,128]{4,3,2,1,0:T(8,128)} fusion(f32[1,2,12,128,128]{4,3,2,1,0:T(8,128)S(1)} %fusion.82, f32[1,2,4,128,128]{4,3,2,1,0:T(8,128)} %copy-done.11, f32[1,2,4,128,128]{4,3,2,1,0:T(8,128)} %copy-done.9, f32[1,2,20,136,136]{4,3,2,1,0:T(8,128)} %select_maximum_fusion, f32[1,1,12,128,128]{4,3,2,1,0:T(8,128)} %copy-done.4, ...), kind=kLoop, calls=%fused_computation.47 | loop fusion | flops 16121856 | bytes 31719424 | tf_op jit(solution)/shard_map/add | solution.py:64
  116.0 1.6 fusion.270
  117.8 0.7 fusion.77
  118.5 1.1 fusion.95
  119.7 1.0 fusion.111
  120.7 1.1 convolution_negate_fusion
  121.8 1.0 fusion.109
  122.9 1.0 fusion.79
  123.9 1.0 fusion.78
  124.9 1.3 pad_maximum_fusion.6
  126.2 1.3 dynamic-slice
  128.5 854.5 %all-reduce.6.cloned.1.call-done = f32[128,2,12,128]{3,0,2,1:T(8,128)} async-done(((f32[128,2,12,128]{3,0,2,1:T(8,128)}), f32[128,2,12,128]{3,0,2,1:T(8,128)}) %all-reduce.6.cloned.1.call-update) | async-done | bytes 1572880
  983.0 0.9 constant_dynamic-slice_fusion
  984.1 1.0 reshape.287
  985.1 4.7 all-to-all-start
  989.8 5.7 all-to-all-done
  995.5 0.5 broadcast.348
  996.0 0.7 reduce
  996.7 0.4 reshape.288
  1000.7 0.9 reshape.289
  1001.5 3.3 all-to-all-start.1
  1005.4 5.1 all-to-all-done.1
  1010.5 0.7 reduce.1
  1012.6 0.4 convolution_add_fusion.1
  1013.0 0.4 convolution_subtract_fusion.2
  1013.5 1.4 fusion.187
  1014.9 1.4 fusion.81
  1016.3 1.4 copy.59
  1017.7 436.1 %reduce-scatter.3.cloned.1.call-done = f32[12,2,128]{2,0,1:T(8,128)} async-done(((f32[12,128,128]{2,0,1:T(8,128)}), f32[12,2,128]{2,0,1:T(8,128)}) %reduce-scatter.3.cloned.1.call-update) | async-done | bytes 12304 | tf_op jit(solution)/shard_map/reduce_scatter | solution.py:159
  1453.8 1.3 copy.60
  (64 shorter events, 7.7 us)
Async XLA Ops:
  7.2 4.8 copy-start
  7.2 975.8 %all-reduce.6.cloned.1.call-start = ((), (), s32[]{:S(2)}) async-start(), calls=%async_computation.4 | async-start | bytes 3145728
  8.6 3.3 collective-permute-start.1
  10.4 5.5 collective-permute-start
  12.3 1.3 copy-start.1
  26.8 11.3 copy-start.7
  26.9 12.6 collective-permute-start.2
  28.3 11.3 collective-permute-start.3
  39.5 4.0 copy-start.8
  39.6 3.9 copy-start.10
  71.9 0.9 copy-start.2
  71.9 1.2 copy-start.4
  73.1 11.0 collective-permute-start.4
  74.4 10.4 collective-permute-start.5
  84.1 4.5 copy-start.9
  84.8 3.9 copy-start.11
  116.0 1.7 copy-start.3
  116.0 1.8 copy-start.5
  118.5 2.2 copy-start.6
  985.1 10.4 all-to-all-start
  1001.5 9.0 all-to-all-start.1
  1004.9 448.9 %reduce-scatter.3.cloned.1.call-start = ((), (), s32[]{:S(2)}) async-start(), calls=%async_computation.3 | async-start | bytes 1064960 | tf_op jit(solution)/shard_map/reduce_scatter | solution.py:159
Sparse Core Ops, SparseCore 0:
  126.3 856.5 all-reduce.5
  1017.9 435.8 reduce-scatter.2
where the time goes:
time: 1480 us; the launch traced here: 1460 us
  waiting for transfers between devices  1300 us (88%)
  other arithmetic  81.5 us (6%)
  starting transfers between devices  33 us (2%)
  between operations  15.9 us (1%)
    unnamed x3, waiting for transfers between devices  855 us
    reduce_scatter x1, waiting for transfers between devices, body(): hartree = lax.psum_scatter(share, 'orb', scatter_dimension=1, tiled=True)  436 us
    add x3, other arithmetic, next_term(): applied = -0.5 * laplacian_rows(padded) + potential_rows * center  62.5 us
  transfers between devices with their start and end apart: 10, of which 8 were waited for; matrix products, arithmetic and copies ran while one was open for 0% of the time, Pallas kernels for 0%

commit v1 on v0

v1 whole, which is shorter than its diff:
```python
import functools
import math

import jax
import jax.numpy as jnp
import numpy as np
from jax import lax
from jax.experimental import pallas as pl
from jax.experimental.pallas import tpu as pltpu
from jax.sharding import PartitionSpec as P

MESH = pl.DeviceIdType.MESH
HIGHEST = lax.Precision.HIGHEST
SPACING = 0.4
TIME_STEP = 0.03
STENCIL = (-205.0 / 72.0, 8.0 / 5.0, -1.0 / 5.0, 8.0 / 315.0, -1.0 / 560.0)
COEF = tuple(-0.5 * c / (SPACING * SPACING) for c in STENCIL)


def real_basis(n):
    grid = np.arange(n)
    rows = np.zeros((n, n))
    for k in range(n):
        m = (k + 1) // 2
        angle = 2.0 * np.pi * ((m * grid) % n) / n
        wave = np.cos(angle) if (k % 2 == 1 or k == 0) else np.sin(angle)
        rows[k] = wave * (np.sqrt(1.0 / n) if m in (0, n // 2) else np.sqrt(2.0 / n))
    return rows


def band(n):
    out = np.zeros((n, n))
    for r in range(1, 5):
        out += COEF[r] * (np.eye(n, k=r) + np.eye(n, k=-r))
    return out


def squares_of(n):
    m = (np.arange(n) + 1) // 2
    return (m * (2.0 * math.pi / (n * SPACING))) ** 2


def dot(a, b):
    return jnp.dot(a, b, precision=HIGHEST, preferred_element_type=jnp.float32)


def orbitals_kernel(dims, occ_ref, orb_ref, pot_ref, dz_ref, dy_ref, new_ref, rho_ref, buf, send, recv, load):
    doms, planes, total_orbs = dims
    last = 4 + planes
    d = lax.axis_index("dom")
    odd = lax.rem(d, 2)
    fast_id = d + 1 - 2 * odd
    slow_id = d - 1 + 2 * odd
    has_slow = jnp.logical_and(slow_id >= 0, slow_id < doms)
    base_fast = (1 - odd) * (planes - 4)
    base_slow = odd * (planes - 4)

    barrier = pltpu.get_barrier_semaphore()
    pl.semaphore_signal(barrier, inc=1, device_id={"dom": fast_id}, device_id_type=MESH)

    @pl.when(has_slow)
    def _():
        pl.semaphore_signal(barrier, inc=1, device_id={"dom": slow_id}, device_id_type=MESH)

    loads = [
        pltpu.make_async_copy(orb_ref.at[0, c], buf.at[0, c, pl.ds(4, planes)], load.at[c]) for c in range(2)
    ]
    for copy in loads:
        copy.start()

    @pl.when(has_slow)
    def _():
        pl.semaphore_wait(barrier, 2)

    @pl.when(jnp.logical_not(has_slow))
    def _():
        pl.semaphore_wait(barrier, 1)

    def halo(k, c, side):
        base = base_slow if side else base_fast
        dst = jnp.where(odd == (0 if side else 1), last, 0)
        if k == 0:
            src = orb_ref.at[0, c, pl.ds(base, 4)]
        else:
            src = buf.at[k, c, pl.ds(4 + base, 4)]
        return pltpu.make_async_remote_copy(
            src_ref=src,
            dst_ref=buf.at[k, c, pl.ds(dst, 4)],
            send_sem=send.at[k, c, side],
            recv_sem=recv.at[k, c, side],
            device_id={"dom": slow_id if side else fast_id},
            device_id_type=MESH,
        )

    def start(k, c, side):
        if side:

            @pl.when(has_slow)
            def _():
                halo(k, c, side).start()

        else:
            halo(k, c, side).start()

    def arrived(k, c, side):
        if side:

            @pl.when(has_slow)
            def _():
                halo(k, c, side).wait_recv()

        else:
            halo(k, c, side).wait_recv()

    for c in range(2):
        start(0, c, 1)
        start(0, c, 0)

    @pl.when(jnp.logical_not(has_slow))
    def _():
        edge = odd * last
        for k in range(3):
            for c in range(2):
                buf[k, c, pl.ds(edge, 4)] = jnp.zeros((4,) + buf.shape[3:], jnp.float32)

    def step(k, c, x):
        f = buf[k, c, 4 + x]
        high = f.astype(jnp.bfloat16)
        low = (f - high.astype(jnp.float32)).astype(jnp.bfloat16)
        h = jnp.dot(jnp.concatenate([high, low], axis=1), dz_ref[...], preferred_element_type=jnp.float32)
        h = h + jnp.dot(dy_ref[...], jnp.concatenate([high, low], axis=0), preferred_element_type=jnp.float32)
        h = h + (3.0 * COEF[0] + pot_ref[x]) * f
        for r in range(1, 5):
            h = h + COEF[r] * (buf[k, c, 4 + x + r] + buf[k, c, 4 + x - r])
        sign = 1.0 if (k + c) % 2 else -1.0
        return (sign * TIME_STEP / (k + 1)) * h

    weight = occ_ref[0] * (1.0 / math.sqrt(total_orbs))

    def sweep(k, c, base, count):
        def body(i, carry):
            x = base + i
            out = step(k, c, x)
            if k < 2:
                buf[k + 1, c, 4 + x] = out
            elif c == 0:
                new_ref[0, 1, x] = ((buf[0, 1, 4 + x] + buf[1, 0, 4 + x]) + buf[2, 1, 4 + x]) + out
            else:
                real = ((buf[0, 0, 4 + x] + buf[1, 1, 4 + x]) + buf[2, 0, 4 + x]) + out
                new_ref[0, 0, x] = real
                imag = new_ref[0, 1, x]
                rho_ref[x] = weight * (real * real + imag * imag)
            return carry

        lax.fori_loop(0, count, body, 0)

    def edges(k, c):
        for side in range(2):
            arrived(k, c, side)
            sweep(k, c, base_slow if side else base_fast, 4)
            if k < 2:
                start(k + 1, c, side)

    for c in range(2):
        loads[c].wait()
        sweep(0, c, 4, planes - 8)
    edges(0, 0)
    sweep(1, 0, 4, planes - 8)
    edges(0, 1)
    sweep(1, 1, 4, planes - 8)
    edges(1, 0)
    edges(1, 1)
    sweep(2, 0, 4, planes - 8)
    sweep(2, 1, 4, planes - 8)
    edges(2, 0)
    edges(2, 1)
    for k in range(3):
        for c in range(2):
            halo(k, c, 0).wait_send()

            @pl.when(has_slow)
            def _():
                halo(k, c, 1).wait_send()


def hartree_kernel(
    dims,
    rho_ref,
    wy_ref,
    iy_ref,
    rz_ref,
    rzt_ref,
    rx_ref,
    rxt_ref,
    qx_ref,
    qz_ref,
    out_ref,
    m1,
    r1,
    s1,
    r2,
    s2,
    r3,
    xs,
    y3,
    r4,
    m5,
    r5,
    s5,
    r6,
    send1,
    recv1,
    send2,
    recv2,
    send3,
    recv3,
    send4,
    recv4,
    send5,
    recv5,
    send6,
    recv6,
):
    A, B, C, D, planes, ny, nz = dims
    half = planes // 2
    groups = B * C
    keep = ny // groups
    rows_a = ny // A
    rows_own = ny // (A * groups)
    line = A * D
    stride = line // keep
    orb = lax.axis_index("orb")
    dom = lax.axis_index("dom")
    a = orb // groups
    b = lax.rem(orb // C, B)
    c = lax.rem(orb, C)
    me = a * D + dom

    def along(axis, offset):
        if axis == 0:
            return a * groups + lax.rem(b + offset, B) * C + c
        return a * groups + b * C + lax.rem(c + offset, C)

    def on_line(place):
        return (place // D) * groups + b * C + c, lax.rem(place, D)

    size = (B, C)
    mine = (b, c)
    barrier = pltpu.get_barrier_semaphore()
    for axis in range(2):
        for o in range(1, size[axis]):
            pl.semaphore_signal(barrier, inc=1, device_id={"orb": along(axis, o)}, device_id_type=MESH)

    def greet(o, carry):
        place = on_line(lax.rem(me + o, line))
        pl.semaphore_signal(barrier, inc=1, device_id={"orb": place[0], "dom": place[1]}, device_id_type=MESH)
        return carry

    lax.fori_loop(1, line, greet, 0)

    def forward(x, carry):
        m1[x] = dot(wy_ref[0], rho_ref[x])
        m1[half + x] = dot(wy_ref[1], rho_ref[half + x])
        return carry

    lax.fori_loop(0, half, forward, 0)
    pl.semaphore_wait(barrier, B - 1 + C - 1 + line - 1)

    def exchange(src, dst, sends, recvs, h, axis, o, count, pre):
        peer = lax.rem(mine[axis] + o, size[axis])
        return pltpu.make_async_remote_copy(
            src_ref=src(peer),
            dst_ref=dst,
            send_sem=sends.at[h, o - 1],
            recv_sem=recvs.at[h, o - 1],
            device_id={"orb": along(axis, o)},
            device_id_type=MESH,
        )

    copies1 = []
    for h in range(2):
        axis = h
        big = ny // size[axis]
        for o in range(1, size[axis]):
            copies1.append(
                exchange(
                    lambda p, h=h, big=big: m1.at[pl.ds(h * half, half), pl.ds(pl.multiple_of(p * big, 8), big)],
                    r1.at[h, o - 1],
                    send1,
                    recv1,
                    h,
                    axis,
                    o,
                    None,
                    None,
                )
            )
    for copy in copies1:
        copy.start()
    copies2 = []
    at = 0
    for h in range(2):
        axis = h
        big = ny // size[axis]
        own = pl.ds(pl.multiple_of(mine[axis] * big, 8), big)
        total = m1[h * half : (h + 1) * half, own]
        for o in range(1, size[axis]):
            copies1[at].wait_recv()
            at += 1
            total = total + r1[h, o - 1]
        s1[h] = total
        other = 1 - h
        for o in range(1, size[other]):
            copy = exchange(
                lambda p, h=h: s1.at[h, :, pl.ds(pl.multiple_of(p * keep, 8), keep)],
                r2.at[h, o - 1],
                send2,
                recv2,
                h,
                other,
                o,
                None,
                None,
            )
            copy.start()
            copies2.append(copy)
    at = 0
    for h in range(2):
        other = 1 - h
        own = pl.ds(pl.multiple_of(mine[other] * keep, 8), keep)
        total = s1[h, :, own]
        for o in range(1, size[other]):
            copies2[at].wait_recv()
            at += 1
            total = total + r2[h, o - 1]
        for x in range(half):
            s2[:, h * half + x, :] = total[x]

    def to_solver(j):
        place = on_line(j * stride)
        return pltpu.make_async_remote_copy(
            src_ref=s2.at[j],
            dst_ref=r3.at[me],
            send_sem=send3.at[j],
            recv_sem=recv3.at[me],
            device_id={"orb": place[0], "dom": place[1]},
            device_id_type=MESH,
        )

    for j in range(keep):

        @pl.when(me != j * stride)
        def _():
            to_solver(j).start()

        @pl.when(me == j * stride)
        def _():
            r3[me] = s2[j]

    def to_slab(place):
        where = on_line(place)
        slab = lax.rem(place, D)
        return pltpu.make_async_remote_copy(
            src_ref=y3.at[slab],
            dst_ref=r4.at[me // stride],
            send_sem=send4.at[place],
            recv_sem=recv4.at[me // stride],
            device_id={"orb": where[0], "dom": where[1]},
            device_id_type=MESH,
        )

    def from_line(place):
        where = on_line(place)
        return pltpu.make_async_remote_copy(
            src_ref=s2.at[0],
            dst_ref=r3.at[place],
            send_sem=send3.at[0],
            recv_sem=recv3.at[place],
            device_id={"orb": where[0], "dom": where[1]},
            device_id_type=MESH,
        )

    @pl.when(lax.rem(me, stride) == 0)
    def _():
        def landed(o, carry):
            from_line(lax.rem(me + o, line)).wait_recv()
            return carry

        lax.fori_loop(1, line, landed, 0)
        for slab in range(D):
            piece = r3[slab]
            for q in range(1, A):
                piece = piece + r3[q * D + slab]
            xs[slab * planes : (slab + 1) * planes, :] = piece
        modes = dot(rx_ref[...], dot(xs[...], rzt_ref[...]))
        wave = (b * C + c) * keep + me // stride
        m = ((wave + 1) // 2).astype(jnp.float32) * (2.0 * math.pi / (ny * SPACING))
        squares = (qx_ref[...] + m * m) + qz_ref[...]
        positive = squares > 0.0
        solved = modes * jnp.where(positive, 4.0 * math.pi / jnp.where(positive, squares, 1.0), 0.0)
        xs[...] = dot(dot(rxt_ref[...], solved), rz_ref[...])
        for slab in range(D):
            y3[slab] = xs[slab * planes : (slab + 1) * planes, :]
        r4[me // stride] = y3[dom]

        def give(o, carry):
            to_slab(lax.rem(me + o, line)).start()
            return carry

        lax.fori_loop(1, line, give, 0)

    def from_solver(j):
        where = on_line(j * stride)
        return pltpu.make_async_remote_copy(
            src_ref=y3.at[0],
            dst_ref=r4.at[j],
            send_sem=send4.at[0],
            recv_sem=recv4.at[j],
            device_id={"orb": where[0], "dom": where[1]},
            device_id_type=MESH,
        )

    for j in range(keep):

        @pl.when(me != j * stride)
        def _():
            from_solver(j).wait_recv()

    first = pl.ds(pl.multiple_of((b * C + c) * keep, 8), keep)
    for h in range(2):
        table = iy_ref[h, first, :]
        for x in range(half):
            rows = r4[:, h * half + x, :]
            m5[h * half + x] = lax.dot_general(
                table, rows, (((0,), (0,)), ((), ())), precision=HIGHEST, preferred_element_type=jnp.float32
            )

    copies5 = []
    for h in range(2):
        axis = h
        big = rows_a // size[axis]
        for o in range(1, size[axis]):
            copy = exchange(
                lambda p, h=h, big=big: m5.at[
                    pl.ds(h * half, half), pl.ds(pl.multiple_of(a * rows_a + p * big, 8), big)
                ],
                r5.at[h, o - 1],
                send5,
                recv5,
                h,
                axis,
                o,
                None,
                None,
            )
            copy.start()
            copies5.append(copy)
    copies6 = []
    at = 0
    for h in range(2):
        axis = h
        other = 1 - h
        big = rows_a // size[axis]
        total = m5[h * half : (h + 1) * half, pl.ds(pl.multiple_of(a * rows_a + mine[axis] * big, 8), big)]
        for o in range(1, size[axis]):
            copies5[at].wait_recv()
            at += 1
            total = total + r5[h, o - 1]
        for p in range(size[other]):
            s5[h, p] = total[:, p * rows_own : (p + 1) * rows_own]
        for o in range(1, size[other]):
            copy = exchange(lambda p, h=h: s5.at[h, p], r6.at[h, o - 1], send6, recv6, h, other, o, None, None)
            copy.start()
            copies6.append(copy)
    at = 0
    for h in range(2):
        other = 1 - h
        total = s5[h, mine[other]]
        for o in range(1, size[other]):
            copies6[at].wait_recv()
            at += 1
            total = total + r6[h, o - 1]
        out_ref[h * half : (h + 1) * half] = total

    for copy in copies1 + copies2 + copies5 + copies6:
        copy.wait_send()
    for j in range(keep):

        @pl.when(me != j * stride)
        def _():
            to_solver(j).wait_send()

    @pl.when(lax.rem(me, stride) == 0)
    def _():
        def gone(o, carry):
            to_slab(lax.rem(me + o, line)).wait_send()
            return carry

        lax.fori_loop(1, line, gone, 0)


def factors(orbs):
    return {64: (4, 4, 4), 8: (2, 2, 2)}[orbs]


def body(orbitals, occupations, potential):
    groups = lax.axis_size("orb")
    doms = lax.axis_size("dom")
    A, B, C = factors(groups)
    planes, ny, nz = potential.shape
    nx = planes * doms
    half = planes // 2
    f32 = jnp.float32
    vmem = pl.BlockSpec(memory_space=pltpu.VMEM)
    dma = pltpu.SemaphoreType.DMA

    dz = band(nz)
    dy = band(ny)
    new, rho = pl.pallas_call(
        functools.partial(orbitals_kernel, (doms, planes, orbitals.shape[0] * groups)),
        out_shape=(jax.ShapeDtypeStruct(orbitals.shape, f32), jax.ShapeDtypeStruct(potential.shape, f32)),
        in_specs=[pl.BlockSpec(memory_space=pltpu.SMEM), pl.BlockSpec(memory_space=pl.ANY), vmem, vmem, vmem],
        out_specs=(vmem, vmem),
        scratch_shapes=[
            pltpu.VMEM((3, 2, planes + 8, ny, nz), f32),
            dma((3, 2, 2)),
            dma((3, 2, 2)),
            dma((2,)),
        ],
        compiler_params=pltpu.CompilerParams(
            collective_id=0, has_side_effects=True, vmem_limit_bytes=40 * 2**20
        ),
    )(
        occupations,
        orbitals,
        potential,
        jnp.asarray(np.concatenate([dz, dz], axis=0), jnp.bfloat16),
        jnp.asarray(np.concatenate([dy, dy], axis=1), jnp.bfloat16),
    )

    ry = real_basis(ny)
    rz = real_basis(nz)
    rx = real_basis(nx)
    keep = ny // (B * C)
    rows_own = ny // groups
    swapped = ry.reshape(B, C, keep, ny).transpose(1, 0, 2, 3).reshape(ny, ny)
    back = ry.reshape(ny, A, B, C, rows_own).transpose(0, 1, 3, 2, 4).reshape(ny, ny)
    dims = (A, B, C, doms, planes, ny, nz)
    line = A * doms
    scratch = [
        pltpu.VMEM((planes, ny, nz), f32),
        pltpu.VMEM((2, B - 1, half, ny // B, nz), f32),
        pltpu.VMEM((2, half, ny // B, nz), f32),
        pltpu.VMEM((2, B - 1, half, keep, nz), f32),
        pltpu.VMEM((keep, planes, nz), f32),
        pltpu.VMEM((line, planes, nz), f32),
        pltpu.VMEM((nx, nz), f32),
        pltpu.VMEM((doms, planes, nz), f32),
        pltpu.VMEM((keep, planes, nz), f32),
        pltpu.VMEM((planes, ny, nz), f32),
        pltpu.VMEM((2, B - 1, half, ny // (A * B), nz), f32),
        pltpu.VMEM((2, B, half, rows_own, nz), f32),
        pltpu.VMEM((2, B - 1, half, rows_own, nz), f32),
        dma((2, B - 1)),
        dma((2, B - 1)),
        dma((2, B - 1)),
        dma((2, B - 1)),
        dma((keep,)),
        dma((line,)),
        dma((line,)),
        dma((keep,)),
        dma((2, B - 1)),
        dma((2, B - 1)),
        dma((2, B - 1)),
        dma((2, B - 1)),
    ]
    tables = [
        np.stack([ry, swapped]),
        np.stack([ry, back]),
        rz,
        rz.T,
        rx,
        rx.T,
        squares_of(nx)[:, None] * np.ones((1, nz)),
        squares_of(nz)[None, :],
    ]
    hartree = pl.pallas_call(
        functools.partial(hartree_kernel, dims),
        out_shape=jax.ShapeDtypeStruct((planes, rows_own, nz), f32),
        in_specs=[vmem] * 9,
        out_specs=vmem,
        scratch_shapes=scratch,
        compiler_params=pltpu.CompilerParams(
            collective_id=1, has_side_effects=True, vmem_limit_bytes=40 * 2**20
        ),
    )(rho, *[jnp.asarray(t, f32) for t in tables])
    return (new, hartree)


def solution(mesh):
    return jax.shard_map(
        body,
        mesh=mesh,
        in_specs=(P("orb", None, "dom", None, None), P("orb"), P("dom", None, None)),
        out_specs=(P("orb", None, "dom", None, None), P("dom", "orb", None)),
        check_vma=False,
    )
```

time: 1480 us -> 84.9 us (0.06); the launches traced: 1460 us -> 83.6 us
  waiting for transfers between devices: 1300 us -> 0 us
  other arithmetic: 81.5 us -> 0 us
  Pallas kernels: 0 us -> 76.2 us
  starting transfers between devices: 33 us -> 0 us
    unnamed x3 -> x0, waiting for transfers between devices: 855 us -> none
    reduce_scatter x1 -> x0, waiting for transfers between devices: 436 us -> none  [body(): hartree = lax.psum_scatter(share, 'orb', scatter_dimension=1, tiled=True)]
    pallas_call x0 -> x2, Pallas kernels: none -> 76.2 us  [the longest x1 58.3 us: body(): pl.pallas_call(functools.partial(hartree_kernel, dims), out_shape=jax.Sha...]
    add x5 -> x0, other arithmetic: 63.3 us -> none  [the longest x3 62.5 us: next_term(): applied = -0.5 * laplacian_rows(padded) + potential_rows * center]
    ppermute x6 -> x0, starting transfers between devices: 24.6 us -> none  [the longest x3 20.6 us: with_halo(): lax.ppermute(tail, axis, [(i, (i + 1) % count) for i in range(ends)])]
  transfers between devices with their start and end apart: 10 -> 0, of which waited for: 8 -> 0; matrix products, arithmetic and copies ran while one was open for 0% -> 0% of each run, Pallas kernels for 0% -> 0%
where the time goes in v1:
time: 84.9 us; the launch traced here: 83.6 us
  Pallas kernels  76.2 us (90%)
  local copies, waits for them, and re-layouts  6 us (7%)
  between operations  1.42 us (2%)
    pallas_call x1, Pallas kernels, body(): pl.pallas_call(functools.partial(hartree_kernel, dims), out_shape=jax.Sha...  58.3 us
    pallas_call x1, Pallas kernels, body(): pl.pallas_call(functools.partial(orbitals_kernel, (doms, planes, orbitals...  17.9 us
    unnamed x26, local copies, waits for them, and re-layouts  6 us

profile of v1, /device:TPU:6, one launch (start us, length us, event | category | flops | bytes accessed | tf_op | source)
XLA Modules:
  0.0 83.6 jit_solution(15536776064333721926)
XLA Ops:
  0.6 0.0 copy-start.11
  1.3 0.0 copy-start
  1.3 1.4 %copy-done = f32[1,2,12,128,128]{4,3,2,1,0:T(8,128)S(1)} copy-done((f32[1,2,12,128,128]{4,3,2,1,0:T(8,128)S(1)}, f32[1,2,12,128,128]{4,3,2,1,0:T(8,128)}, u32[]{:S(2)}) %copy-start) | copy-done | bytes 1572888
  2.7 0.0 copy-start.1
  2.7 1.1 %copy-done.1 = f32[12,128,128]{2,1,0:T(8,128)S(1)} copy-done((f32[12,128,128]{2,1,0:T(8,128)S(1)}, f32[12,128,128]{2,1,0:T(8,128)}, u32[]{:S(2)}) %copy-start.1) | copy-done | bytes 786456
  3.8 0.0 copy-start.4
  3.8 0.8 %copy-done.4 = bf16[128,256]{1,0:T(8,128)(2,1)S(1)} copy-done((bf16[128,256]{1,0:T(8,128)(2,1)S(1)}, bf16[128,256]{1,0:T(8,128)(2,1)}, u32[]{:S(2)}) %copy-start.4) | copy-done | bytes 65560
  4.7 0.0 copy-start.7
  4.7 0.8 %copy-done.7 = bf16[256,128]{1,0:T(8,128)(2,1)S(1)} copy-done((bf16[256,128]{1,0:T(8,128)(2,1)S(1)}, bf16[256,128]{1,0:T(8,128)(2,1)}, u32[]{:S(2)}) %copy-start.7) | copy-done | bytes 65560
  5.5 0.0 copy-start.2
  5.5 0.0 copy-start.3
  5.5 0.0 copy-start.5
  5.5 0.0 copy-start.6
  5.5 0.0 copy-start.8
  5.5 0.0 copy-start.9
  5.6 0.0 copy-start.10
  5.6 17.9 %shard_map.140 = (f32[1,2,12,128,128]{4,3,2,1,0:T(8,128)S(1)}, f32[12,128,128]{2,1,0:T(8,128)S(1)}) custom-call(f32[1]{0:T(128)S(6)} %copy.17.occ_ref, f32[1,2,12,128,128]{4,3,2,1,0:T(8,128)S(1)} %copy-done, f32[12,128,128]{2,1,0:T(8,128)S(1)} %copy-done.1, bf16[256,128]{1,0:T(8,128)(2,1)S(1)} %copy-done.7, bf16[128,256]{1,0:T(8,128)(2,1)S(1)} %copy-done.4), custom_call_target="tpu_custom_call" | custom-call | tf_op jit(solution)/shard_map/pallas_call | solution.py:519
  23.5 0.0 copy-done.11
  23.5 0.0 copy-done.2
  23.5 0.0 copy-done.3
  23.5 0.0 copy-done.5
  23.5 0.0 copy-done.6
  23.5 0.0 copy-done.8
  23.5 0.0 copy-done.9
  23.5 0.0 copy-done.10
  23.6 58.3 %shard_map.141 = f32[12,2,128]{2,1,0:T(2,128)S(1)} custom-call(f32[12,128,128]{2,1,0:T(8,128)S(1)} %get-tuple-element.5.rho_ref, f32[2,128,128]{2,1,0:T(8,128)S(1)} %copy-done.3, f32[2,128,128]{2,1,0:T(8,128)S(1)} %copy-done.2, f32[128,128]{1,0:T(8,128)S(1)} %copy-done.6, f32[128,128]{1,0:T(8,128)S(1)} %copy-done.5, f32[96,96]{1,0:T(8,128)S(1)} %copy-done.10, ...), custom_call_target="tpu_custom_call" | custom-call | tf_op jit(solution)/shard_map/pallas_call | solution.py:587
  81.9 1.1 %copy.18 = f32[1,2,12,128,128]{4,3,2,1,0:T(8,128)} copy(f32[1,2,12,128,128]{4,3,2,1,0:T(8,128)S(1)} %get-tuple-element.8) | data formatting | bytes 3145728
  83.0 0.6 copy.19
Async XLA Ops:
  0.6 22.8 %copy-start.11 = (f32[1,128]{1,0:T(1,128)S(1)}, f32[1,128]{1,0:T(1,128)}, u32[]{:S(2)}) copy-start(f32[1,128]{1,0:T(1,128)} %constant.29.clone.qz_ref) | copy-start | bytes 1540
  1.3 1.4 %copy-start = (f32[1,2,12,128,128]{4,3,2,1,0:T(8,128)S(1)}, f32[1,2,12,128,128]{4,3,2,1,0:T(8,128)}, u32[]{:S(2)}) copy-start(f32[1,2,12,128,128]{4,3,2,1,0:T(8,128)} %orb_ref.1) | copy-start | bytes 4718596
  2.7 1.1 %copy-start.1 = (f32[12,128,128]{2,1,0:T(8,128)S(1)}, f32[12,128,128]{2,1,0:T(8,128)}, u32[]{:S(2)}) copy-start(f32[12,128,128]{2,1,0:T(8,128)} %pot_ref.1) | copy-start | bytes 2359300
  3.8 0.8 %copy-start.4 = (bf16[128,256]{1,0:T(8,128)(2,1)S(1)}, bf16[128,256]{1,0:T(8,128)(2,1)}, u32[]{:S(2)}) copy-start(bf16[128,256]{1,0:T(8,128)(2,1)} %constant.21.clone.dy_ref) | copy-start | bytes 196612
  4.7 0.8 %copy-start.7 = (bf16[256,128]{1,0:T(8,128)(2,1)S(1)}, bf16[256,128]{1,0:T(8,128)(2,1)}, u32[]{:S(2)}) copy-start(bf16[256,128]{1,0:T(8,128)(2,1)} %constant.20.clone.dz_ref) | copy-start | bytes 196612
  5.5 18.0 %copy-start.2 = (f32[2,128,128]{2,1,0:T(8,128)S(1)}, f32[2,128,128]{2,1,0:T(8,128)}, u32[]{:S(2)}) copy-start(f32[2,128,128]{2,1,0:T(8,128)} %constant.23.clone.iy_ref) | copy-start | bytes 393220
  5.5 18.0 %copy-start.3 = (f32[2,128,128]{2,1,0:T(8,128)S(1)}, f32[2,128,128]{2,1,0:T(8,128)}, u32[]{:S(2)}) copy-start(f32[2,128,128]{2,1,0:T(8,128)} %constant.22.clone.wy_ref) | copy-start | bytes 393220
  5.5 18.0 %copy-start.5 = (f32[128,128]{1,0:T(8,128)S(1)}, f32[128,128]{1,0:T(8,128)}, u32[]{:S(2)}) copy-start(f32[128,128]{1,0:T(8,128)} %constant.25.clone.rzt_ref) | copy-start | bytes 196612
  5.5 18.0 %copy-start.6 = (f32[128,128]{1,0:T(8,128)S(1)}, f32[128,128]{1,0:T(8,128)}, u32[]{:S(2)}) copy-start(f32[128,128]{1,0:T(8,128)} %constant.24.clone.rz_ref) | copy-start | bytes 196612
  5.5 18.0 %copy-start.8 = (f32[96,128]{1,0:T(8,128)S(1)}, f32[96,128]{1,0:T(8,128)}, u32[]{:S(2)}) copy-start(f32[96,128]{1,0:T(8,128)} %constant.28.clone.qx_ref) | copy-start | bytes 147460
  5.5 18.0 %copy-start.9 = (f32[96,96]{1,0:T(8,128)S(1)}, f32[96,96]{1,0:T(8,128)}, u32[]{:S(2)}) copy-start(f32[96,96]{1,0:T(8,128)} %constant.27.clone.rxt_ref) | copy-start | bytes 110596
  5.6 18.0 %copy-start.10 = (f32[96,96]{1,0:T(8,128)S(1)}, f32[96,96]{1,0:T(8,128)}, u32[]{:S(2)}) copy-start(f32[96,96]{1,0:T(8,128)} %constant.26.clone.rx_ref) | copy-start | bytes 110596

commit v2 on v0

v2 whole, which is shorter than its diff:
```python
import functools
import math

import jax
import jax.numpy as jnp
import numpy as np
from jax import lax
from jax.experimental import pallas as pl
from jax.experimental.pallas import tpu as pltpu
from jax.sharding import PartitionSpec as P

MESH = pl.DeviceIdType.MESH
HIGHEST = lax.Precision.HIGHEST
SPACING = 0.4
TIME_STEP = 0.03
STENCIL = (-205.0 / 72.0, 8.0 / 5.0, -1.0 / 5.0, 8.0 / 315.0, -1.0 / 560.0)
COEF = tuple(-0.5 * c / (SPACING * SPACING) for c in STENCIL)


def real_basis(n):
    grid = np.arange(n)
    rows = np.zeros((n, n))
    for k in range(n):
        m = (k + 1) // 2
        angle = 2.0 * np.pi * ((m * grid) % n) / n
        wave = np.cos(angle) if (k % 2 == 1 or k == 0) else np.sin(angle)
        rows[k] = wave * (np.sqrt(1.0 / n) if m in (0, n // 2) else np.sqrt(2.0 / n))
    return rows


def band(n):
    out = np.zeros((n, n))
    for r in range(1, 5):
        out += COEF[r] * (np.eye(n, k=r) + np.eye(n, k=-r))
    return out


def squares_of(n):
    m = (np.arange(n) + 1) // 2
    return (m * (2.0 * math.pi / (n * SPACING))) ** 2


def dot(a, b):
    return jnp.dot(a, b, precision=HIGHEST, preferred_element_type=jnp.float32)


def wrap(value, n):
    return jnp.where(value >= n, value - n, value)


def layout(nx, ny, nz):
    rows, places = 0, {}
    for name, count in (
        ("wy0", ny),
        ("wy1", ny),
        ("iy0", ny),
        ("iy1", ny),
        ("rz", nz),
        ("rzt", nz),
        ("rx", nx),
        ("rxt", nx),
        ("qx", nx),
        ("qz", 8),
    ):
        places[name] = (rows, count)
        rows += -(-count // 8) * 8
    return places, rows


def kernel(
    dims,
    occ_ref,
    orb_ref,
    pot_hbm,
    dz_hbm,
    dy_hbm,
    table_hbm,
    new_ref,
    out_ref,
    buf,
    res,
    pot_ref,
    dz_ref,
    dy_ref,
    tab,
    m1,
    r1,
    s1,
    r2,
    s2,
    r3,
    xs,
    y3,
    r4,
    m5,
    r5,
    s5,
    r6,
    load,
    store,
    token,
    send0,
    recv0,
    send1,
    recv1,
    send2,
    recv2,
    send3,
    recv3,
    send4,
    recv4,
    send5,
    recv5,
    send6,
    recv6,
):
    A, B, C, D, planes, ny, nz = dims
    nx = planes * D
    half = planes // 2
    groups = B * C
    keep = ny // groups
    rows_a = ny // A
    rows_own = ny // (A * groups)
    line = A * D
    stride = line // keep
    last = 4 + planes
    places, _ = layout(nx, ny, nz)

    orb = lax.axis_index("orb")
    dom = lax.axis_index("dom")
    a = orb // groups
    b = lax.rem(orb // C, B)
    c = lax.rem(orb, C)
    inner = orb - a * groups
    me = a * D + dom
    odd = lax.rem(dom, 2)
    fast_id = dom + 1 - 2 * odd
    slow_id = dom - 1 + 2 * odd
    has_slow = jnp.logical_and(slow_id >= 0, slow_id < D)
    base_fast = (1 - odd) * (planes - 4)
    base_slow = odd * (planes - 4)
    size = (B, C)
    mine = (b, c)

    def along(axis, offset):
        if axis == 0:
            return {"orb": a * groups + wrap(b + offset, B) * C + c}
        return {"orb": a * groups + b * C + wrap(c + offset, C)}

    def on_line(offset):
        slab = dom + offset % D
        over = (slab >= D).astype(jnp.int32)
        slab = slab - D * over
        block = wrap(a + offset // D + over, A)
        return {"orb": block * groups + inner, "dom": slab}, block * D + slab, slab

    barrier = pltpu.get_barrier_semaphore()
    for offset in (1, line - 1):
        pl.semaphore_signal(barrier, inc=1, device_id=on_line(offset)[0], device_id_type=MESH)
    for axis in range(2):
        for o in range(1, size[axis]):
            pl.semaphore_signal(barrier, inc=1, device_id=along(axis, o), device_id_type=MESH)
    loads = [
        pltpu.make_async_copy(orb_ref.at[0, 0], buf.at[0, 0, pl.ds(4, planes)], load.at[0]),
        pltpu.make_async_copy(orb_ref.at[0, 1], buf.at[0, 1, pl.ds(4, planes)], load.at[1]),
        pltpu.make_async_copy(dz_hbm, dz_ref, load.at[2]),
        pltpu.make_async_copy(dy_hbm, dy_ref, load.at[3]),
        pltpu.make_async_copy(pot_hbm, pot_ref, load.at[4]),
        pltpu.make_async_copy(table_hbm, tab, load.at[5]),
    ]
    for copy in loads:
        copy.start()
    pl.semaphore_wait(barrier, B + C)

    def halo(k, ch, side):
        base = base_slow if side else base_fast
        dst = jnp.where(odd == (0 if side else 1), last, 0)
        if k == 0:
            src = orb_ref.at[0, ch, pl.ds(base, 4)]
        else:
            src = buf.at[k, ch, pl.ds(4 + base, 4)]
        return pltpu.make_async_remote_copy(
            src_ref=src,
            dst_ref=buf.at[k, ch, pl.ds(dst, 4)],
            send_sem=send0.at[k, ch, side],
            recv_sem=recv0.at[k, ch, side],
            device_id={"dom": slow_id if side else fast_id},
            device_id_type=MESH,
        )

    def guarded(side, act):
        if side:
            pl.when(has_slow)(act)
        else:
            act()

    def start(k, ch, side):
        guarded(side, lambda: halo(k, ch, side).start())

    def arrived(k, ch, side):
        guarded(side, lambda: halo(k, ch, side).wait_recv())

    for ch in range(2):
        start(0, ch, 1)
    for ch in range(2):
        start(0, ch, 0)

    def tell(r):
        reach = 2**r
        for offset in (reach, line - reach):
            pl.semaphore_signal(token.at[r], inc=1, device_id=on_line(offset)[0], device_id_type=MESH)

    def told(r):
        pl.semaphore_wait(token.at[r], 2)

    rounds = max(1, (line // 2).bit_length() - 1)
    tell(0)

    @pl.when(jnp.logical_not(has_slow))
    def _():
        edge = odd * last
        for k in range(3):
            for ch in range(2):
                buf[k, ch, pl.ds(edge, 4)] = jnp.zeros((4, ny, nz), jnp.float32)

    def step(k, ch, x):
        f = buf[k, ch, 4 + x]
        high = f.astype(jnp.bfloat16)
        low = (f - high.astype(jnp.float32)).astype(jnp.bfloat16)
        h = jnp.dot(jnp.concatenate([high, low], axis=1), dz_ref[...], preferred_element_type=jnp.float32)
        h = h + jnp.dot(dy_ref[...], jnp.concatenate([high, low], axis=0), preferred_element_type=jnp.float32)
        h = h + (3.0 * COEF[0] + pot_ref[x]) * f
        for r in range(1, 5):
            h = h + COEF[r] * (buf[k, ch, 4 + x + r] + buf[k, ch, 4 + x - r])
        sign = 1.0 if (k + ch) % 2 else -1.0
        return (sign * TIME_STEP / (k + 1)) * h

    weight = occ_ref[0] * (1.0 / math.sqrt(A * groups))

    def sweep(k, ch, base):
        def body(i, carry):
            x = base + i
            out = step(k, ch, x)
            if k < 2:
                buf[k + 1, ch, 4 + x] = out
            elif ch == 0:
                res[1, x] = ((buf[0, 1, 4 + x] + buf[1, 0, 4 + x]) + buf[2, 1, 4 + x]) + out
            else:
                real = ((buf[0, 0, 4 + x] + buf[1, 1, 4 + x]) + buf[2, 0, 4 + x]) + out
                res[0, x] = real
                imag = res[1, x]
                m1[i // 2, base // 2 + lax.rem(i, 2)] = weight * (real * real + imag * imag)
            return carry

        lax.fori_loop(0, 4, body, 0, unroll=4)
        if k == 2 and ch == 1:
            for h in range(2):
                first, count = places["wy%d" % h]
                for i in range(2):
                    at = base // 2 + i
                    m1[h, at] = dot(tab[first : first + count, :ny], m1[h, at])

    def middle(k, ch):
        for base in range(4, planes - 4, 4):
            sweep(k, ch, base)

    def edge_of(k, ch, side):
        arrived(k, ch, side)
        sweep(k, ch, base_slow if side else base_fast)
        if k < 2:
            start(k + 1, ch, side)

    loads[2].wait()
    loads[3].wait()
    loads[4].wait()
    for ch in range(2):
        loads[ch].wait()
        middle(0, ch)
    for ch in range(2):
        edge_of(0, ch, 0)
    told(0)
    if rounds > 1:
        tell(1)
    edge_of(0, 0, 1)
    middle(1, 0)
    edge_of(1, 0, 0)
    edge_of(0, 1, 1)
    middle(1, 1)
    edge_of(1, 1, 0)
    if rounds > 1:
        told(1)
    if rounds > 2:
        tell(2)
    edge_of(1, 0, 1)
    edge_of(1, 1, 1)
    if rounds > 2:
        told(2)
    if rounds > 3:
        tell(3)
    loads[5].wait()
    for ch in range(2):
        middle(2, ch)
        edge_of(2, ch, 0)

    early = planes // 2 - 2
    starts = ((1 - odd) * 2, odd * early)
    counts = (early, 2)

    def first_hop(t, h, o):
        axis = h
        big = ny // size[axis]
        peer = wrap(mine[axis] + o, size[axis])
        part = pl.ds(starts[t], counts[t])
        return pltpu.make_async_remote_copy(
            src_ref=m1.at[h, part, pl.ds(pl.multiple_of(peer * big, 8), big)],
            dst_ref=r1.at[h, o - 1, part],
            send_sem=send1.at[t, h, o - 1],
            recv_sem=recv1.at[t, h, o - 1],
            device_id=along(axis, o),
            device_id_type=MESH,
        )

    def second_hop(t, h, o):
        axis = 1 - h
        peer = wrap(mine[axis] + o, size[axis])
        part = pl.ds(starts[t], counts[t])
        return pltpu.make_async_remote_copy(
            src_ref=s1.at[h, part, pl.ds(pl.multiple_of(peer * keep, 8), keep)],
            dst_ref=r2.at[h, o - 1, part],
            send_sem=send2.at[t, h, o - 1],
            recv_sem=recv2.at[t, h, o - 1],
            device_id=along(axis, o),
            device_id_type=MESH,
        )

    def offsets(n):
        return sorted(range(1, n), key=lambda o: -min(o, n - o))

    def each(t, make, act):
        for h in range(2):
            axis = h if make in (first_hop, third_hop) else 1 - h
            for o in offsets(size[axis]):
                act(make(t, h, o))

    def begin(copy):
        copy.start()

    def left(copy):
        copy.wait_send()

    def third_hop(t, h, o):
        axis = h
        big = rows_a // size[axis]
        peer = wrap(mine[axis] + o, size[axis])
        return pltpu.make_async_remote_copy(
            src_ref=m5.at[h, :, pl.ds(pl.multiple_of(a * rows_a + peer * big, 8), big)],
            dst_ref=r5.at[h, o - 1],
            send_sem=send5.at[h, o - 1],
            recv_sem=recv5.at[h, o - 1],
            device_id=along(axis, o),
            device_id_type=MESH,
        )

    def fourth_hop(t, h, o):
        axis = 1 - h
        peer = wrap(mine[axis] + o, size[axis])
        return pltpu.make_async_remote_copy(
            src_ref=s5.at[h, peer],
            dst_ref=r6.at[h, o - 1],
            send_sem=send6.at[h, o - 1],
            recv_sem=recv6.at[h, o - 1],
            device_id=along(axis, o),
            device_id_type=MESH,
        )

    each(0, first_hop, begin)
    edge_of(2, 0, 1)
    pltpu.make_async_copy(res.at[1], new_ref.at[0, 1], store.at[1]).start()
    edge_of(2, 1, 1)
    each(1, first_hop, begin)
    pltpu.make_async_copy(res.at[0], new_ref.at[0, 0], store.at[0]).start()
    for t in range(2):
        part = pl.ds(starts[t], counts[t])
        for h in range(2):
            axis = h
            big = ny // size[axis]
            total = m1[h, part, pl.ds(pl.multiple_of(mine[axis] * big, 8), big)]
            for o in range(1, size[axis]):
                first_hop(t, h, o).wait_recv()
                total = total + r1[h, o - 1, part]
            s1[h, part] = total
            for o in offsets(size[1 - h]):
                second_hop(t, h, o).start()
    each(0, second_hop, lambda copy: copy.wait_recv())
    each(1, second_hop, lambda copy: copy.wait_recv())
    for h in range(2):
        axis = 1 - h
        total = s1[h, :, pl.ds(pl.multiple_of(mine[axis] * keep, 8), keep)]
        for o in range(1, size[axis]):
            total = total + r2[h, o - 1]
        for p in range(half):
            s2[:, (p // 2) * 4 + 2 * h + p % 2, :] = total[p]

    if rounds > 3:
        told(3)
    own = me // stride
    solver = lax.rem(me, stride) == 0

    def to_solver(i):
        j = wrap(own + i, keep)
        place = j * stride
        block = place // D
        return pltpu.make_async_remote_copy(
            src_ref=s2.at[j],
            dst_ref=r3.at[me],
            send_sem=send3.at[i],
            recv_sem=recv3.at[me],
            device_id={"orb": block * groups + inner, "dom": place - block * D},
            device_id_type=MESH,
        )

    for i in sorted(range(1, keep), key=lambda i: -min(i, keep - i)):
        to_solver(i).start()

    @pl.when(jnp.logical_not(solver))
    def _():
        to_solver(0).start()

    def to_slab(offset):
        device, place, slab = on_line(offset)
        return pltpu.make_async_remote_copy(
            src_ref=y3.at[slab],
            dst_ref=r4.at[own],
            send_sem=send4.at[offset],
            recv_sem=recv4.at[own],
            device_id=device,
            device_id_type=MESH,
        )

    far_first = sorted(range(1, line), key=lambda o: -min(o // 2, line // 2 - o // 2))

    @pl.when(solver)
    def _():
        r3[me] = s2[own]
        for offset in range(1, line):
            device, place, slab = on_line(offset)
            pltpu.make_async_remote_copy(
                src_ref=s2.at[0],
                dst_ref=r3.at[place],
                send_sem=send3.at[0],
                recv_sem=recv3.at[place],
                device_id=device,
                device_id_type=MESH,
            ).wait_recv()
        for slab in range(D):
            piece = r3[slab]
            for q in range(1, A):
                piece = piece + r3[q * D + slab]
            xs[slab * planes : (slab + 1) * planes, :] = piece

        def table(name):
            first, count = places[name]
            return tab[first : first + count, :]

        modes = dot(table("rx")[:, :nx], dot(xs[...], table("rzt")))
        wave = inner * keep + own
        m = ((wave + 1) // 2).astype(jnp.float32) * (2.0 * math.pi / (ny * SPACING))
        squares = (table("qx") + m * m) + table("qz")[:1]
        positive = squares > 0.0
        solved = modes * jnp.where(positive, 4.0 * math.pi / jnp.where(positive, squares, 1.0), 0.0)
        xs[...] = dot(dot(table("rxt")[:, :nx], solved), table("rz"))
        for slab in range(D):
            y3[slab] = xs[slab * planes : (slab + 1) * planes, :]
        for offset in far_first:
            to_slab(offset).start()
        r4[own] = y3[dom]

    def from_solver(i):
        j = wrap(own + i, keep)
        place = j * stride
        block = place // D
        return pltpu.make_async_remote_copy(
            src_ref=y3.at[0],
            dst_ref=r4.at[j],
            send_sem=send4.at[0],
            recv_sem=recv4.at[j],
            device_id={"orb": block * groups + inner, "dom": place - block * D},
            device_id_type=MESH,
        )

    for i in range(1, keep):
        from_solver(i).wait_recv()

    @pl.when(jnp.logical_not(solver))
    def _():
        from_solver(0).wait_recv()

    for h in range(2):
        table = tab[pl.ds(pl.multiple_of(places["iy%d" % h][0] + inner * keep, 8), keep), :]
        for p in range(half):
            rows = r4[:, (p // 2) * 4 + 2 * h + p % 2, :]
            m5[h, p] = lax.dot_general(
                table, rows, (((0,), (0,)), ((), ())), precision=HIGHEST, preferred_element_type=jnp.float32
            )[:ny]
        for o in offsets(size[h]):
            third_hop(0, h, o).start()
    for h in range(2):
        axis = h
        big = rows_a // size[axis]
        total = m5[h, :, pl.ds(pl.multiple_of(a * rows_a + mine[axis] * big, 8), big)]
        for o in range(1, size[axis]):
            third_hop(0, h, o).wait_recv()
            total = total + r5[h, o - 1]
        for p in range(size[1 - h]):
            s5[h, p] = total[:, p * rows_own : (p + 1) * rows_own]
        for o in offsets(size[1 - h]):
            fourth_hop(0, h, o).start()
    for h in range(2):
        axis = 1 - h
        total = s5[h, mine[axis]]
        for o in range(1, size[axis]):
            fourth_hop(0, h, o).wait_recv()
            total = total + r6[h, o - 1]
        for p in range(half):
            out_ref[(p // 2) * 4 + 2 * h + p % 2] = total[p]

    for k in range(3):
        for ch in range(2):
            for side in range(2):
                guarded(side, lambda k=k, ch=ch, side=side: halo(k, ch, side).wait_send())
    for t in range(2):
        each(t, first_hop, left)
        each(t, second_hop, left)
    each(0, third_hop, left)
    each(0, fourth_hop, left)
    for i in range(1, keep):
        to_solver(i).wait_send()

    @pl.when(jnp.logical_not(solver))
    def _():
        to_solver(0).wait_send()

    @pl.when(solver)
    def _():
        for offset in far_first:
            to_slab(offset).wait_send()

    for part in range(2):
        pltpu.make_async_copy(res.at[part], new_ref.at[0, part], store.at[part]).wait()


def factors(orbs):
    return {64: (4, 4, 4), 8: (2, 2, 2)}[orbs]


def body(orbitals, occupations, potential):
    groups = lax.axis_size("orb")
    doms = lax.axis_size("dom")
    A, B, C = factors(groups)
    planes, ny, nz = potential.shape
    nx = planes * doms
    half = planes // 2
    keep = ny // (B * C)
    rows_own = ny // groups
    line = A * doms
    f32 = jnp.float32
    vmem = pl.BlockSpec(memory_space=pltpu.VMEM)
    hbm = pl.BlockSpec(memory_space=pltpu.HBM)
    dma = pltpu.SemaphoreType.DMA

    dz = band(nz)
    dy = band(ny)
    ry = real_basis(ny)
    rz = real_basis(nz)
    rx = real_basis(nx)
    swapped = ry.reshape(B, C, keep, ny).transpose(1, 0, 2, 3).reshape(ny, ny)
    back = ry.reshape(ny, A, B, C, rows_own).transpose(0, 1, 3, 2, 4).reshape(ny, ny)
    places, rows = layout(nx, ny, nz)
    table = np.zeros((rows, max(ny, nz, nx)), np.float32)
    for name, value in (
        ("wy0", ry),
        ("wy1", swapped),
        ("iy0", ry),
        ("iy1", back),
        ("rz", rz),
        ("rzt", rz.T),
        ("rx", rx),
        ("rxt", rx.T),
        ("qx", squares_of(nx)[:, None] * np.ones((1, nz))),
        ("qz", squares_of(nz)[None, :]),
    ):
        first = places[name][0]
        table[first : first + value.shape[0], : value.shape[1]] = value
    scratch = [
        pltpu.VMEM((3, 2, planes + 8, ny, nz), f32),
        pltpu.VMEM((2, planes, ny, nz), f32),
        pltpu.VMEM((planes, ny, nz), f32),
        pltpu.VMEM((2 * nz, nz), jnp.bfloat16),
        pltpu.VMEM((ny, 2 * ny), jnp.bfloat16),
        pltpu.VMEM(table.shape, f32),
        pltpu.VMEM((2, half, ny, nz), f32),
        pltpu.VMEM((2, B - 1, half, ny // B, nz), f32),
        pltpu.VMEM((2, half, ny // B, nz), f32),
        pltpu.VMEM((2, B - 1, half, keep, nz), f32),
        pltpu.VMEM((keep, planes, nz), f32),
        pltpu.VMEM((line, planes, nz), f32),
        pltpu.VMEM((nx, nz), f32),
        pltpu.VMEM((doms, planes, nz), f32),
        pltpu.VMEM((keep, planes, nz), f32),
        pltpu.VMEM((2, half, ny, nz), f32),
        pltpu.VMEM((2, B - 1, half, ny // (A * B), nz), f32),
        pltpu.VMEM((2, B, half, rows_own, nz), f32),
        pltpu.VMEM((2, B - 1, half, rows_own, nz), f32),
        dma((6,)),
        dma((2,)),
        pltpu.SemaphoreType.REGULAR((4,)),
        dma((3, 2, 2)),
        dma((3, 2, 2)),
        dma((2, 2, B - 1)),
        dma((2, 2, B - 1)),
        dma((2, 2, B - 1)),
        dma((2, 2, B - 1)),
        dma((keep,)),
        dma((line,)),
        dma((line,)),
        dma((keep,)),
        dma((2, B - 1)),
        dma((2, B - 1)),
        dma((2, B - 1)),
        dma((2, B - 1)),
    ]
    return pl.pallas_call(
        functools.partial(kernel, (A, B, C, doms, planes, ny, nz)),
        out_shape=(
            jax.ShapeDtypeStruct(orbitals.shape, f32),
            jax.ShapeDtypeStruct((planes, rows_own, nz), f32),
        ),
        in_specs=[pl.BlockSpec(memory_space=pltpu.SMEM)] + [hbm] * 5,
        out_specs=(hbm, vmem),
        scratch_shapes=scratch,
        compiler_params=pltpu.CompilerParams(
            collective_id=0, has_side_effects=True, vmem_limit_bytes=60 * 2**20
        ),
    )(
        occupations,
        orbitals,
        potential,
        jnp.asarray(np.concatenate([dz, dz], axis=0), jnp.bfloat16),
        jnp.asarray(np.concatenate([dy, dy], axis=1), jnp.bfloat16),
        jnp.asarray(table),
    )


def solution(mesh):
    return jax.shard_map(
        body,
        mesh=mesh,
        in_specs=(P("orb", None, "dom", None, None), P("orb"), P("dom", None, None)),
        out_specs=(P("orb", None, "dom", None, None), P("dom", "orb", None)),
        check_vma=False,
    )
```

time: 1480 us -> 69.5 us (0.05); the launches traced: 1460 us -> 69.2 us
  waiting for transfers between devices: 1300 us -> 0 us
  other arithmetic: 81.5 us -> 0 us
  Pallas kernels: 0 us -> 64.6 us
  starting transfers between devices: 33 us -> 0 us
    unnamed x3 -> x0, waiting for transfers between devices: 855 us -> none
    reduce_scatter x1 -> x0, waiting for transfers between devices: 436 us -> none  [body(): hartree = lax.psum_scatter(share, 'orb', scatter_dimension=1, tiled=True)]
    pallas_call x0 -> x1, Pallas kernels: none -> 64.6 us  [body(): pl.pallas_call(functools.partial(kernel, (A, B, C, doms, planes, ny, nz))...]
    add x5 -> x0, other arithmetic: 63.3 us -> none  [the longest x3 62.5 us: next_term(): applied = -0.5 * laplacian_rows(padded) + potential_rows * center]
    ppermute x6 -> x0, starting transfers between devices: 24.6 us -> none  [the longest x3 20.6 us: with_halo(): lax.ppermute(tail, axis, [(i, (i + 1) % count) for i in range(ends)])]
  transfers between devices with their start and end apart: 10 -> 0, of which waited for: 8 -> 0; matrix products, arithmetic and copies ran while one was open for 0% -> 0% of each run, Pallas kernels for 0% -> 0%
where the time goes in v2:
time: 69.5 us; the launch traced here: 69.2 us
  Pallas kernels  64.6 us (93%)
  local copies, waits for them, and re-layouts  3.31 us (5%)
  between operations  1.29 us (2%)
    pallas_call x1, Pallas kernels, body(): pl.pallas_call(functools.partial(kernel, (A, B, C, doms, planes, ny, nz))...  64.6 us
    unnamed x4, local copies, waits for them, and re-layouts  3.31 us

profile of v2, /device:TPU:6, one launch (start us, length us, event | category | flops | bytes accessed | tf_op | source)
XLA Modules:
  0.0 69.2 jit_solution(17188803892596068587)
XLA Ops:
  1.3 64.6 %shard_map.77 = (f32[1,2,12,128,128]{4,3,2,1,0:T(8,128)}, f32[12,2,128]{2,1,0:T(2,128)}) custom-call(f32[1]{0:T(128)S(6)} %copy.10.occ_ref, f32[1,2,12,128,128]{4,3,2,1,0:T(8,128)} %orb_ref.1, f32[12,128,128]{2,1,0:T(8,128)} %pot_hbm.1, bf16[256,128]{1,0:T(8,128)(2,1)} %constant.6.clone.dz_hbm, bf16[128,256]{1,0:T(8,128)(2,1)} %constant.7.clone.dy_hbm, ...), custom_call_target="tpu_custom_call" | custom-call | tf_op jit(solution)/shard_map/pallas_call | solution.py:632
  65.9 0.0 copy-start
  65.9 2.7 %copy.11 = f32[1,2,12,128,128]{4,3,2,1,0:T(8,128)} copy(f32[1,2,12,128,128]{4,3,2,1,0:T(8,128)} %get-tuple-element.4) | data formatting | bytes 3145728
  68.6 0.0 copy-done
  68.6 0.6 copy.12
Async XLA Ops:
  65.9 2.7 %copy-start = (f32[12,2,128]{2,1,0:T(2,128)S(1)}, f32[12,2,128]{2,1,0:T(2,128)}, u32[]{:S(2)}) copy-start(f32[12,2,128]{2,1,0:T(2,128)} %get-tuple-element.5) | copy-start | bytes 36868

commit v3 on v2

--- a/solution.py
+++ b/solution.py
@@ -292,15 +292,12 @@
     if rounds > 2:
         tell(2)
     edge_of(1, 0, 1)
+    middle(2, 0)
+    edge_of(2, 0, 0)
     edge_of(1, 1, 1)
-    if rounds > 2:
-        told(2)
-    if rounds > 3:
-        tell(3)
     loads[5].wait()
-    for ch in range(2):
-        middle(2, ch)
-        edge_of(2, ch, 0)
+    middle(2, 1)
+    edge_of(2, 1, 0)
 
     early = planes // 2 - 2
     starts = ((1 - odd) * 2, odd * early)
@@ -374,6 +371,10 @@
         )
 
     each(0, first_hop, begin)
+    if rounds > 2:
+        told(2)
+    if rounds > 3:
+        tell(3)
     edge_of(2, 0, 1)
     pltpu.make_async_copy(res.at[1], new_ref.at[0, 1], store.at[1]).start()
     edge_of(2, 1, 1)
@@ -547,6 +548,29 @@
 
     for part in range(2):
         pltpu.make_async_copy(res.at[part], new_ref.at[0, part], store.at[part]).wait()
+
+
+def finish_kernel(new_in, out_in, new_ref, out_ref, held, small, sems):
+    cut = new_in.shape[2] // 4
+    pieces = [(part, pl.ds(q * cut, cut)) for part in range(2) for q in range(4)]
+    count = len(pieces)
+    ins = [
+        pltpu.make_async_copy(new_in.at[0, part, piece], held.at[part, piece], sems.at[0, i])
+        for i, (part, piece) in enumerate(pieces)
+    ]
+    outs = [
+        pltpu.make_async_copy(held.at[part, piece], new_ref.at[0, part, piece], sems.at[1, i])
+        for i, (part, piece) in enumerate(pieces)
+    ]
+    ins.append(pltpu.make_async_copy(out_in, small, sems.at[0, count]))
+    outs.append(pltpu.make_async_copy(small, out_ref, sems.at[1, count]))
+    for copy in ins:
+        copy.start()
+    for first, second in zip(ins, outs):
+        first.wait()
+        second.start()
+    for copy in outs:
+        copy.wait()
 
 
 def factors(orbs):
@@ -629,7 +653,7 @@
         dma((2, B - 1)),
         dma((2, B - 1)),
     ]
-    return pl.pallas_call(
+    new, hartree = pl.pallas_call(
         functools.partial(kernel, (A, B, C, doms, planes, ny, nz)),
         out_shape=(
             jax.ShapeDtypeStruct(orbitals.shape, f32),
@@ -649,6 +673,21 @@
         jnp.asarray(np.concatenate([dy, dy], axis=1), jnp.bfloat16),
         jnp.asarray(table),
     )
+    return pl.pallas_call(
+        finish_kernel,
+        out_shape=(
+            jax.ShapeDtypeStruct(orbitals.shape, f32),
+            jax.ShapeDtypeStruct((planes, rows_own, nz), f32),
+        ),
+        in_specs=[hbm] * 2,
+        out_specs=(hbm, hbm),
+        scratch_shapes=[
+            pltpu.VMEM(orbitals.shape[1:], f32),
+            pltpu.VMEM((planes, rows_own, nz), f32),
+            dma((2, 9)),
+        ],
+        compiler_params=pltpu.CompilerParams(vmem_limit_bytes=60 * 2**20),
+    )(new, hartree)
 
 
 def solution(mesh):

time: 69.5 us -> 68.6 us (0.987)
  local copies, waits for them, and re-layouts: 3.31 us -> 0 us
  Pallas kernels: 64.6 us -> 67 us
    unnamed x4 -> x0, local copies, waits for them, and re-layouts: 3.31 us -> none
    pallas_call x0 -> x1, Pallas kernels: none -> 2.31 us  [body(): pl.pallas_call(finish_kernel, out_shape=(jax.ShapeDtypeStruct(orbitals.sh...]
where the time goes in v3:
time: 68.6 us; the launch traced here: 68.3 us
  Pallas kernels  67 us (98%)
  between operations  1.28 us (2%)
    pallas_call x1, Pallas kernels, body(): pl.pallas_call(functools.partial(kernel, (A, B, C, doms, planes, ny, nz))...  64.7 us
    pallas_call x1, Pallas kernels, body(): pl.pallas_call(finish_kernel, out_shape=(jax.ShapeDtypeStruct(orbitals.sh...  2.31 us

profile of v3, /device:TPU:6, one launch (start us, length us, event | category | flops | bytes accessed | tf_op | source)
XLA Modules:
  0.0 68.3 jit_solution(7383942399930736353)
XLA Ops:
  1.3 64.7 %shard_map.77 = (f32[1,2,12,128,128]{4,3,2,1,0:T(8,128)}, f32[12,2,128]{2,1,0:T(2,128)}) custom-call(f32[1]{0:T(128)S(6)} %copy.8.occ_ref, f32[1,2,12,128,128]{4,3,2,1,0:T(8,128)} %orb_ref.1, f32[12,128,128]{2,1,0:T(8,128)} %pot_hbm.1, bf16[256,128]{1,0:T(8,128)(2,1)} %constant.6.clone.dz_hbm, bf16[128,256]{1,0:T(8,128)(2,1)} %constant.7.clone.dy_hbm, ...), custom_call_target="tpu_custom_call" | custom-call | tf_op jit(solution)/shard_map/pallas_call | solution.py:656
  66.0 2.3 %shard_map.78 = (f32[1,2,12,128,128]{4,3,2,1,0:T(8,128)}, f32[12,2,128]{2,1,0:T(2,128)}) custom-call(f32[1,2,12,128,128]{4,3,2,1,0:T(8,128)} %get-tuple-element.4.new_in, f32[12,2,128]{2,1,0:T(2,128)} %get-tuple-element.5.out_in), custom_call_target="tpu_custom_call" | custom-call | tf_op jit(solution)/shard_map/pallas_call | solution.py:676

commit v4 on v3

--- a/solution.py
+++ b/solution.py
@@ -404,41 +404,57 @@
 
     if rounds > 3:
         told(3)
-    own = me // stride
-    solver = lax.rem(me, stride) == 0
-
-    def to_solver(i):
-        j = wrap(own + i, keep)
-        place = j * stride
+    here = me // stride
+    spot = lax.rem(me, stride)
+    second = spot == stride // 2
+    solver = jnp.logical_or(spot == 0, second)
+    own = jnp.where(second, wrap(here + keep // 2, keep), here)
+
+    def to_solver(s, i):
+        j = wrap(here + i, keep)
+        place = j * stride if s == 0 else wrap(j + keep // 2, keep) * stride + stride // 2
         block = place // D
         return pltpu.make_async_remote_copy(
             src_ref=s2.at[j],
             dst_ref=r3.at[me],
-            send_sem=send3.at[i],
+            send_sem=send3.at[s, i],
             recv_sem=recv3.at[me],
             device_id={"orb": block * groups + inner, "dom": place - block * D},
             device_id_type=MESH,
         )
 
-    for i in sorted(range(1, keep), key=lambda i: -min(i, keep - i)):
-        to_solver(i).start()
-
-    @pl.when(jnp.logical_not(solver))
-    def _():
-        to_solver(0).start()
+    def to_solvers(act):
+        for far in range(keep // 2, -1, -1):
+            for s in range(2):
+                for step_ in sorted({far, (keep - far) % keep}):
+                    i = (step_ + s * (keep // 2)) % keep
+                    if far:
+                        act(to_solver(s, i))
+                    else:
+                        pl.when(spot != s * (stride // 2))(lambda s=s, i=i: act(to_solver(s, i)))
+
+    to_solvers(begin)
 
     def to_slab(offset):
-        device, place, slab = on_line(offset)
-        return pltpu.make_async_remote_copy(
+        place = lax.rem(me + offset + line - jnp.where(second, stride // 2, 0), line)
+        block = place // D
+        slab = place - block * D
+        copy = pltpu.make_async_remote_copy(
             src_ref=y3.at[slab],
             dst_ref=r4.at[own],
-            send_sem=send4.at[offset],
+            send_sem=send4.at[offset + line // 4],
             recv_sem=recv4.at[own],
-            device_id=device,
+            device_id={"orb": block * groups + inner, "dom": slab},
             device_id_type=MESH,
         )
-
-    far_first = sorted(range(1, line), key=lambda o: -min(o // 2, line // 2 - o // 2))
+        return copy, place != me
+
+    far_first = sorted(range(-(line // 4), line // 4), key=lambda o: -abs(o))
+
+    def to_slabs(act):
+        for offset in far_first:
+            copy, other = to_slab(offset)
+            pl.when(other)(lambda copy=copy: act(copy))
 
     @pl.when(solver)
     def _():
@@ -448,7 +464,7 @@
             pltpu.make_async_remote_copy(
                 src_ref=s2.at[0],
                 dst_ref=r3.at[place],
-                send_sem=send3.at[0],
+                send_sem=send3.at[0, 0],
                 recv_sem=recv3.at[place],
                 device_id=device,
                 device_id_type=MESH,
@@ -472,8 +488,7 @@
         xs[...] = dot(dot(table("rxt")[:, :nx], solved), table("rz"))
         for slab in range(D):
             y3[slab] = xs[slab * planes : (slab + 1) * planes, :]
-        for offset in far_first:
-            to_slab(offset).start()
+        to_slabs(begin)
         r4[own] = y3[dom]
 
     def from_solver(i):
@@ -534,17 +549,11 @@
         each(t, second_hop, left)
     each(0, third_hop, left)
     each(0, fourth_hop, left)
-    for i in range(1, keep):
-        to_solver(i).wait_send()
-
-    @pl.when(jnp.logical_not(solver))
-    def _():
-        to_solver(0).wait_send()
+    to_solvers(left)
 
     @pl.when(solver)
     def _():
-        for offset in far_first:
-            to_slab(offset).wait_send()
+        to_slabs(left)
 
     for part in range(2):
         pltpu.make_async_copy(res.at[part], new_ref.at[0, part], store.at[part]).wait()
@@ -644,9 +653,9 @@
         dma((2, 2, B - 1)),
         dma((2, 2, B - 1)),
         dma((2, 2, B - 1)),
-        dma((keep,)),
+        dma((2, keep)),
         dma((line,)),
-        dma((line,)),
+        dma((line // 2,)),
         dma((keep,)),
         dma((2, B - 1)),
         dma((2, B - 1)),

time: 68.6 us -> 67.9 us (0.990)
  no operation moved by 1% of the time
where the time goes in v4:
time: 67.9 us; the launch traced here: 67.7 us
  Pallas kernels  66.5 us (98%)
  between operations  1.28 us (2%)
    pallas_call x1, Pallas kernels, body(): pl.pallas_call(functools.partial(kernel, (A, B, C, doms, planes, ny, nz))...  64.1 us
    pallas_call x1, Pallas kernels, body(): pl.pallas_call(finish_kernel, out_shape=(jax.ShapeDtypeStruct(orbitals.sh...  2.31 us

profile of v4, /device:TPU:6, one launch (start us, length us, event | category | flops | bytes accessed | tf_op | source)
XLA Modules:
  0.0 67.7 jit_solution(12191198161789537847)
XLA Ops:
  1.3 64.1 %shard_map.77 = (f32[1,2,12,128,128]{4,3,2,1,0:T(8,128)}, f32[12,2,128]{2,1,0:T(2,128)}) custom-call(f32[1]{0:T(128)S(6)} %copy.8.occ_ref, f32[1,2,12,128,128]{4,3,2,1,0:T(8,128)} %orb_ref.1, f32[12,128,128]{2,1,0:T(8,128)} %pot_hbm.1, bf16[256,128]{1,0:T(8,128)(2,1)} %constant.6.clone.dz_hbm, bf16[128,256]{1,0:T(8,128)(2,1)} %constant.7.clone.dy_hbm, ...), custom_call_target="tpu_custom_call" | custom-call | tf_op jit(solution)/shard_map/pallas_call | solution.py:665
  65.4 2.3 %shard_map.78 = (f32[1,2,12,128,128]{4,3,2,1,0:T(8,128)}, f32[12,2,128]{2,1,0:T(2,128)}) custom-call(f32[1,2,12,128,128]{4,3,2,1,0:T(8,128)} %get-tuple-element.4.new_in, f32[12,2,128]{2,1,0:T(2,128)} %get-tuple-element.5.out_in), custom_call_target="tpu_custom_call" | custom-call | tf_op jit(solution)/shard_map/pallas_call | solution.py:685
